TPU v7x, 768 devices: a whole 4x8x12 slice. The times are simulated.
768 devices in a mesh: dp: 8 (over y), pack: 12 (over z), mp: 8 (over x, core).
Axes of the slice: x: 4, y: 8, z: 12, core: 2. Of those that a mesh axis runs over, the one named last changes fastest.
Arguments:
- tile_activity: bfloat16 [384, 256, 1536], P(('dp', 'pack'), None, 'mp'), may hold values from -100 to 100
- tokens_per_picture: int32 [384, 4], P(('dp', 'pack')), may hold values from 16 to 128, as said below
- slot_destinations: int32 [384], P(('dp', 'pack')), may hold values from -1 to 23, as said below
- caption_indices: int32 [384, 4], P(('dp', 'pack')), may hold values from 0 to 767, as said below
- attention_projections: bfloat16 [3, 1536, 1536], P(None, None, 'mp'), may hold values from -1 to 1
- caption_vectors: bfloat16 [768, 1536], P(('dp', 'pack'), 'mp'), may hold values from -600 to 600
- score_inverse_heat: float32 [1], replicated, may hold values from 4 to 12
- score_shift: float32 [1], replicated, may hold values from -3 to 0
Outputs:
- image_grads: float32 [768, 1536], P(('dp', 'pack'), 'mp')
- text_grads: float32 [768, 1536], P(('dp', 'pack'), 'mp')
Inputs may be any that keep to these rules, and one draw needn't show every extreme that they name: `slot_destinations`: within one dp index, the block slots of the 12 pack devices name every value 0 .. 23 exactly once; -1 marks an empty slot. No device sends more than 1 block to one destination, and in every dp index some device holds 4 real blocks. `caption_indices`: over the images of non-empty block slots every text index appears exactly once. `tokens_per_picture`: in every block slot the 4 counts sum to 256; exactly one of them is 128 and each other is at least 16.
All inputs are finite; a program needn't handle non-finite values.
Results may differ from a plain program's by a relative error of at most 0.0045.
Values may be sent and summed in bfloat16 or wider, within the bound.
A program may use at most 32 MiB of HBM per device.

v0:
```python
import jax
import jax.numpy as jnp
from jax import lax
from jax.sharding import PartitionSpec as P

HEAD = 64
BLK = 256
IPB = 4
DEST = 2


def normalized_grads(sigmoid_slopes, other_rows, other_scale):
    unit_rows = other_rows.astype(jnp.float32) * other_scale[:, None]
    return jnp.dot(sigmoid_slopes, unit_rows, precision=lax.Precision.HIGHEST)


def pairwise_sigmoid_slopes(
    similarity_products,
    left_norm_factor,
    right_norm_factor,
    matching_pairs,
    smoothing_coefficient,
    logit_offset_value,
):
    pair_logit_matrix = (
        smoothing_coefficient
        * similarity_products
        * left_norm_factor[:, None]
        * right_norm_factor[None, :]
        + logit_offset_value
    )
    signed_pair_labels = jnp.where(matching_pairs, 1.0, -1.0).astype(pair_logit_matrix.dtype)
    return (
        -signed_pair_labels
        * jax.nn.sigmoid(-signed_pair_labels * pair_logit_matrix)
        * smoothing_coefficient
    )


def on_device(
    tile_activity,
    tokens_per_picture,
    slot_destinations,
    caption_indices,
    attention_projections,
    caption_vectors,
    score_inverse_heat,
    score_shift,
):
    pack_index = lax.axis_index("pack")
    slot_ids = jnp.arange(DEST, dtype=jnp.int32)
    block_info = jnp.concatenate(
        [slot_destinations[:, None], tokens_per_picture, caption_indices], axis=1
    )
    arrived, arrived_info = (
        lax.all_gather(tile_activity, "pack", axis=0, tiled=True),
        lax.all_gather(block_info, "pack", axis=0, tiled=True),
    )
    placing = arrived_info[:, 0][None, :] == pack_index * DEST + slot_ids[:, None]
    blocks = jnp.einsum(
        "sb,bpf->spf", placing.astype(jnp.bfloat16), arrived, preferred_element_type=jnp.float32
    ).astype(jnp.bfloat16)
    picked = jnp.sum(placing.astype(jnp.int32)[:, :, None] * arrived_info[None], axis=1)
    image_sizes = picked[:, 1 : 1 + IPB]
    pair_ids = picked[:, 1 + IPB :].reshape(DEST * IPB)
    row_count = DEST * BLK
    local_width = attention_projections.shape[2]
    columns_piece = lax.all_gather(blocks, "mp", axis=2, tiled=True)
    piece_width = columns_piece.shape[2]
    flat_piece = columns_piece.reshape(row_count, piece_width)
    projected = jnp.einsum(
        "rk,ckh->crh", flat_piece, attention_projections, preferred_element_type=jnp.float32
    )
    projected = projected.astype(jnp.bfloat16)
    head_count = local_width // HEAD
    queries = projected[0].reshape(DEST, BLK, head_count, HEAD)
    key_rows = projected[1].reshape(DEST, BLK, head_count, HEAD)
    values = projected[2].reshape(DEST, BLK, head_count, HEAD)
    image_ends = jnp.cumsum(image_sizes, axis=1)
    position = jnp.arange(BLK, dtype=jnp.int32)
    segment = jnp.sum((position[None, None, :] >= image_ends[:, :, None]).astype(jnp.int32), axis=1)
    scores = jnp.einsum(
        "bphe,bqhe->bhpq", queries, key_rows, preferred_element_type=jnp.float32
    ) * HEAD ** (-0.5)
    same_image = segment[:, None, :, None] == segment[:, None, None, :]
    scores = jnp.where(same_image, scores, -1e30)
    row_max = jnp.max(scores, axis=-1, keepdims=True)
    exponent = jnp.exp(scores - row_max)
    probabilities = (exponent / jnp.sum(exponent, axis=-1, keepdims=True)).astype(jnp.bfloat16)
    attended = jnp.einsum(
        "bhpq,bqhe->bphe", probabilities, values, preferred_element_type=jnp.float32
    )
    pooling = (segment[:, None, :] == jnp.arange(IPB, dtype=jnp.int32)[None, :, None]).astype(
        jnp.float32
    )
    pooling = pooling / image_sizes.astype(jnp.float32)[:, :, None]
    pooled = jnp.einsum("bmp,bphe->bmhe", pooling, attended, precision=lax.Precision.HIGHEST)
    embeds = pooled.reshape(DEST * IPB, local_width).astype(jnp.bfloat16)
    smoothing_coefficient = score_inverse_heat[0]
    logit_offset_value = score_shift[0]
    every_text = lax.all_gather(caption_vectors, ("dp", "pack"), axis=0, tiled=True)
    similarity_products = jnp.dot(embeds, every_text.T, preferred_element_type=jnp.float32)
    own_squares = jnp.sum(embeds.astype(jnp.float32) ** 2, axis=1)
    text_squares = jnp.sum(every_text.astype(jnp.float32) ** 2, axis=1)
    similarity_products, own_squares, text_squares = lax.psum(
        (similarity_products, own_squares, text_squares), "mp"
    )
    image_norm_factor = lax.rsqrt(own_squares + 1e-06)
    gathered_text_norm_factor = lax.rsqrt(text_squares + 1e-06)
    text_total = every_text.shape[0]
    matching_pairs = pair_ids[:, None] == jnp.arange(text_total, dtype=jnp.int32)[None, :]
    sigmoid_slopes = pairwise_sigmoid_slopes(
        similarity_products,
        image_norm_factor,
        gathered_text_norm_factor,
        matching_pairs,
        smoothing_coefficient,
        logit_offset_value,
    )
    image_grads = normalized_grads(sigmoid_slopes, every_text, gathered_text_norm_factor)
    partial_grads = normalized_grads(sigmoid_slopes.T, embeds, image_norm_factor)
    text_grads = lax.psum_scatter(partial_grads, ("dp", "pack"), scatter_dimension=0, tiled=True)
    return (image_grads, text_grads)


def solution(mesh):
    return jax.shard_map(
        on_device,
        mesh=mesh,
        in_specs=(
            P(("dp", "pack"), None, "mp"),
            P(("dp", "pack"), None),
            P(("dp", "pack")),
            P(("dp", "pack"), None),
            P(None, None, "mp"),
            P(("dp", "pack"), "mp"),
            P(),
            P(),
        ),
        out_specs=(P(("dp", "pack"), "mp"), P(("dp", "pack"), "mp")),
        check_vma=False,
    )
```

profile of v0, /device:TPU:1, one launch (start us, length us, event | category | flops | bytes accessed | tf_op | source)
XLA Modules:
  0.0 869.1 jit_solution(14420616437906303164)
XLA Ops:
  7.2 0.0 copy-start
  7.2 0.0 all-gather.4.cloned.1.call-start
  7.2 0.7 all-gather.4.cloned.1.call-update
  7.9 0.0 all-gather.6.cloned.1.call-start
  8.0 0.7 copy.32
  8.7 0.8 add_bitcast_fusion
  9.5 27.7 %all-gather = s32[12,4,9]{2,1,0:T(4,128)S(1)} all-gather(s32[1,4,9]{2,1,0:T(4,128)S(1)} %add_bitcast_fusion), channel_id=1, replica_groups=mesh['dp'=8,'pack'=12,'mp'=8] {'pack'}, dimensions={0}, use_global_device_ids=true | all-gather | bytes 1872 | tf_op jit(solution)/shard_map/all_gather | solution.py:57
  37.2 0.1 copy.33
  37.3 0.0 copy-start.1
  37.3 49.1 %all-gather.4.cloned.1.call-done = bf16[48,256,192]{1,2,0:T(8,128)(2,1)} async-done(((bf16[4,256,192]{1,2,0:T(8,128)(2,1)}), bf16[48,256,192]{1,2,0:T(8,128)(2,1)}) %all-gather.4.cloned.1.call-update) | async-done | bytes 4718608 | tf_op jit(solution)/shard_map/all_gather | solution.py:56
  86.4 5.7 fusion.5
  92.1 0.0 all-gather.6.cloned.1.call-update
  92.1 0.0 reduce-scatter.2.cloned.1.call-start
  93.5 0.1 compare_convert_fusion
  93.5 0.2 multiply_reduce_fusion.1
  93.8 0.1 copy.35
  93.9 0.1 eq.69
  94.0 0.1 copy.37
  94.1 0.1 copy.36
  94.2 0.0 copy-done.1
  94.2 54.3 %all_gather.15 = bf16[768,192]{1,0:T(8,128)(2,1)S(1)} all-gather(bf16[8,192]{1,0:T(8,128)(2,1)S(1)} %copy-done.1), channel_id=1, replica_groups=mesh['dp'=8,'pack'=12,'mp'=8] {'dp','pack'}, dimensions={0}, use_global_device_ids=true | all-gather | bytes 297984 | tf_op jit(solution)/shard_map/all_gather | solution.py:101
  148.5 0.1 convert_reduce_fusion
  148.6 0.2 fusion.8
  148.8 0.1 broadcast_compare_fusion
  148.9 0.0 all-gather.6.cloned.1.call-done
  149.0 5.0 copy.39
  153.9 0.0 copy-done
  153.9 2.5 fusion.43
  156.4 0.1 convert_bitcast_fusion
  156.6 0.1 reshape_squeeze.9
  156.6 0.1 reshape_squeeze.11
  156.7 0.1 reshape_squeeze.10
  156.7 1.8 fusion.38
  158.6 1.6 convolution_bitcast_fusion
  160.2 0.6 multiply_reduce_fusion
  160.9 0.1 reduce_sum.51
  161.0 0.1 convert_element_type.56
  161.1 0.2 fusion.44
  161.3 36.3 %all-reduce = (f32[768]{0:T(1024)S(1)}, f32[8,768]{1,0:T(8,128)S(1)}, f32[8]{0:T(128)S(1)}) all-reduce(f32[768]{0:T(1024)S(1)} %fusion.8, f32[8,768]{1,0:T(8,128)S(1)} %fusion.44, f32[8]{0:T(128)S(1)} %reduce_sum.51), channel_id=1, replica_groups=mesh['dp'=8,'pack'=12,'mp'=8] {'mp'}, use_global_device_ids=true, to_apply=%region_9.10 | all-reduce | flops 6920 | bytes 55360 | tf_op jit(solution)/shard_map/psum | solution.py:105
  197.6 1.8 fusion.19
  199.4 0.0 reduce-scatter.2.cloned.1.call-update
  199.4 1.2 fusion.9
  200.6 662.0 %reduce-scatter.2.cloned.1.call-done = f32[8,192]{1,0:T(8,128)} async-done(((f32[768,192]{1,0:T(8,128)}), f32[8,192]{1,0:T(8,128)}) %reduce-scatter.2.cloned.1.call-update) | async-done | bytes 6160 | tf_op jit(solution)/shard_map/reduce_scatter | solution.py:122
  (8 shorter events, 0.1 us)
Async XLA Ops:
  7.2 146.8 %copy-start = (bf16[3,1536,192]{1,2,0:T(8,128)(2,1)S(1)}, bf16[3,1536,192]{1,2,0:T(8,128)(2,1)}, u32[]{:S(2)}) copy-start(bf16[3,1536,192]{1,2,0:T(8,128)(2,1)} %param.12) | copy-start | bytes 5308420
  7.2 79.2 %all-gather.4.cloned.1.call-start = ((), (), s32[]{:S(2)}) async-start(), calls=%async_computation.1 | async-start | bytes 5111808 | tf_op jit(solution)/shard_map/all_gather | solution.py:56
  7.9 141.0 %all-gather.6.cloned.1.call-start = ((), (), s32[]{:S(2)}) async-start(), calls=%async_computation.2 | async-start | bytes 1769472 | tf_op jit(solution)/shard_map/all_gather | solution.py:68
  37.3 56.9 %copy-start.1 = (bf16[8,192]{1,0:T(8,128)(2,1)S(1)}, bf16[8,192]{1,0:T(8,128)(2,1)}, u32[]{:S(2)}) copy-start(bf16[8,192]{1,0:T(8,128)(2,1)} %param.13) | copy-start | bytes 9220
  92.1 770.5 %reduce-scatter.2.cloned.1.call-start = ((), (), s32[]{:S(2)}) async-start(), calls=%async_computation.3 | async-start | bytes 794624 | tf_op jit(solution)/shard_map/reduce_scatter | solution.py:122
Sparse Core Ops, SparseCore 0:
  10.4 75.9 all-gather.3
  92.2 31.8 all-gather.5
  199.5 663.0 reduce-scatter.1
where the time goes:
time: 870 us; the launch traced here: 869 us
  waiting for transfers between devices  712 us (82%)
  blocking collectives  118 us (14%)
  matrix products  15.5 us (2%)
  between operations  15.1 us (2%)
    reduce_scatter x1, waiting for transfers between devices, on_device(): lax.psum_scatter(partial_grads, ('dp', 'pack'), scatter_dimension=0, tile...  662 us
    all_gather x1, blocking collectives, on_device(): lax.all_gather(caption_vectors, ('dp', 'pack'), axis=0, tiled=True)  54.3 us
    all_gather x1, waiting for transfers between devices, on_device(): lax.all_gather(tile_activity, 'pack', axis=0, tiled=True)  49.1 us
    psum x1, blocking collectives, on_device(): lax.psum((similarity_products, own_squares, text_squares), 'mp')  36.3 us
    all_gather x1, blocking collectives, on_device(): lax.all_gather(block_info, 'pack', axis=0, tiled=True)  27.7 us
  transfers between devices with their start and end apart: 3, of which 2 were waited for; matrix products, arithmetic and copies ran while one was open for 0% of the time, Pallas kernels for 0%

commit v1 on v0

v1 whole, which is shorter than its diff:
```python
import functools

import jax
import jax.numpy as jnp
from jax import lax
from jax.experimental import pallas as pl
from jax.experimental.pallas import tpu as pltpu
from jax.sharding import PartitionSpec as P

HEAD = 64
BLK = 256
IPB = 4
DEST = 2
SRC = 4
F32 = jnp.float32
BF16 = jnp.bfloat16
MESH = pl.DeviceIdType.MESH

LABEL_HI, LABEL_LO, PLACE, SQ0, SQ1, SQ2 = 192, 193, 194, 195, 196, 197


def dot(a, b):
    return jnp.dot(a, b, preferred_element_type=F32)


def dot_t(a, b):
    return lax.dot_general(a, b, (((1,), (1,)), ((), ())), preferred_element_type=F32)


def iota(shape, axis):
    return lax.broadcasted_iota(jnp.int32, shape, axis)


def split2(a):
    hi = a.astype(BF16)
    return hi, (a - hi.astype(F32)).astype(BF16)


def kernel(
    n_dp,
    n_pack,
    n_mp,
    tile_hbm,
    sizes_ref,
    dest_ref,
    caption_ref,
    proj_hbm,
    texts_ref,
    heat_ref,
    shift_ref,
    image_out,
    text_out,
    raw,
    proj,
    rows,
    w_main,
    w_low,
    w_high,
    qx,
    kx,
    pooled,
    text_rows,
    pack_rows,
    sims,
    own_text,
    own_image,
    text_terms,
    image_terms,
    load_sem,
    x_send,
    x_recv,
    t_send,
    t_recv,
    e_send,
    e_recv,
    s_send,
    s_recv,
    ty_send,
    ty_recv,
    iz_send,
    iz_recv,
):
    g, p, m = lax.axis_index("dp"), lax.axis_index("pack"), lax.axis_index("mp")
    chips = n_mp // 2
    chip, core = m // 2, m % 2
    right = ((chip + 1) % chips) * 2 + core
    left = ((chip + chips - 1) % chips) * 2 + core
    far = ((chip + 2) % chips) * 2 + core
    twin = chip * 2 + 1 - core
    width = texts_ref.shape[1]

    load_tile = pltpu.make_async_copy(tile_hbm, raw, load_sem.at[0])
    load_proj = pltpu.make_async_copy(proj_hbm, proj, load_sem.at[1])
    load_tile.start()
    load_proj.start()

    barrier = pltpu.get_barrier_semaphore()
    for d in range(1, n_mp):
        pl.semaphore_signal(barrier, inc=1, device_id={"mp": (m + d) % n_mp}, device_id_type=MESH)
    for d in range(1, n_dp):
        pl.semaphore_signal(barrier, inc=1, device_id={"dp": (g + d) % n_dp}, device_id_type=MESH)
    for d in range(1, n_pack):
        pl.semaphore_signal(
            barrier, inc=1, device_id={"pack": (p + d) % n_pack}, device_id_type=MESH
        )

    load_tile.wait()
    half = BLK // 2
    for s in range(SRC):
        rows[s, m, 0:BLK, :] = raw[s, :, 0:128]
        tail = jnp.concatenate(
            [raw[s, 0:half, 128:192].astype(F32), raw[s, half:BLK, 128:192].astype(F32)], axis=1
        )
        rows[s, m, BLK : BLK + half, :] = tail.astype(BF16)
    text_rows[g] = jnp.zeros((8, 256), F32)
    text_rows[g, :, 0:width] = texts_ref[...].astype(F32)

    pl.semaphore_wait(barrier, n_mp + n_dp + n_pack - 3)

    def remote(src, dst, send, recv, where):
        return pltpu.make_async_remote_copy(
            src_ref=src,
            dst_ref=dst,
            send_sem=send,
            recv_sem=recv,
            device_id=where,
            device_id_type=MESH,
        )

    mid = (BLK + half) // 2

    def own_to_right(s):
        return remote(rows.at[s, m], rows.at[s, m], x_send.at[s, 0], x_recv.at[s, 0], {"mp": right})

    def own_to_left(s):
        return remote(rows.at[s, m], rows.at[s, m], x_send.at[s, 1], x_recv.at[s, 1], {"mp": left})

    def own_to_twin(s):
        return remote(rows.at[s, m], rows.at[s, m], x_send.at[s, 2], x_recv.at[s, 2], {"mp": twin})

    def pass_right(s):
        part = rows.at[s, left, pl.ds(0, mid)]
        return remote(part, part, x_send.at[s, 3], x_recv.at[s, 3], {"mp": right})

    def pass_left(s):
        part = rows.at[s, right, pl.ds(mid, mid)]
        return remote(part, part, x_send.at[s, 4], x_recv.at[s, 4], {"mp": left})

    def share(s, whose, k):
        part = rows.at[s, whose]
        return remote(part, part, x_send.at[s, k], x_recv.at[s, k], {"mp": twin})

    def got(s, k, part):
        return remote(part, part, x_send.at[s, k], x_recv.at[s, k], {"mp": twin})

    for s in range(SRC):
        own_to_right(s).start()
        own_to_left(s).start()
        own_to_twin(s).start()

    def text_copy(d):
        return remote(
            text_rows.at[g], text_rows.at[g], t_send.at[d], t_recv.at[g], {"dp": (g + d) % n_dp}
        )

    for d in range(1, n_dp):
        text_copy(d).start()

    load_proj.wait()
    w_low[...] = jnp.zeros_like(w_low)
    w_high[...] = jnp.zeros_like(w_high)
    for c in range(3):
        for k in range(n_mp):
            w_main[c, k * 128 : k * 128 + 128, :] = proj[c, k * width : k * width + 128, :]
            rest = proj[c, k * width + 128 : k * width + 192, :]
            w_low[c, k * 128 : k * 128 + 64, :] = rest
            w_high[c, k * 128 + 64 : k * 128 + 128, :] = rest
    pooled[...] = jnp.zeros_like(pooled)

    def pass_on(s):
        got(s, 0, rows.at[s, left]).wait_recv()
        pass_right(s).start()
        share(s, left, 5).start()
        got(s, 1, rows.at[s, right]).wait_recv()
        pass_left(s).start()
        share(s, right, 6).start()

    lane = iota((BLK, 256), 1)

    def attend(s):
        e1 = sizes_ref[s, 0]
        e2 = e1 + sizes_ref[s, 1]
        e3 = e2 + sizes_ref[s, 2]

        def image_of(position):
            return (
                (position >= e1).astype(jnp.int32)
                + (position >= e2).astype(jnp.int32)
                + (position >= e3).astype(jnp.int32)
            )

        same = image_of(iota((BLK, 256), 0)) == lane - width
        extra = (lane >= width) & (lane < width + IPB)
        qx[...] = jnp.where(extra & same, -1e30, 0.0).astype(BF16)
        kx[...] = jnp.where(extra & jnp.logical_not(same), 1.0, 0.0).astype(BF16)

        main = jnp.concatenate([rows[s, k, 0:BLK, :] for k in range(n_mp)], axis=1)
        tails = jnp.concatenate([rows[s, k, BLK : BLK + half, :] for k in range(n_mp)], axis=1)

        def project(c):
            return dot(main, w_main[c]) + jnp.concatenate(
                [dot(tails, w_low[c]), dot(tails, w_high[c])], axis=0
            )

        qx[:, 0:width] = (project(0) * HEAD**-0.5).astype(BF16)
        kx[:, 0:width] = project(1).astype(BF16)
        values = project(2).astype(BF16)
        keys = kx[...]
        queries = qx[...]

        row16 = iota((SRC * IPB, BLK), 0)
        member = (row16 // IPB == s) & (row16 % IPB == image_of(iota((SRC * IPB, BLK), 1)))
        member = jnp.where(member, 1.0, 0.0).astype(BF16)
        weights = []
        for h in range(width // HEAD):
            keep = ((lane >= h * HEAD) & (lane < (h + 1) * HEAD)) | (lane >= width)
            scores = dot_t(keys, jnp.where(keep, queries, jnp.zeros_like(queries)))
            exponent = jnp.exp(scores - jnp.max(scores, axis=0, keepdims=True))
            inverse = 1.0 / jnp.sum(exponent, axis=0, keepdims=True)
            weights.append(dot_t(member, (exponent * inverse).astype(BF16)))
        hi, lo = split2(jnp.concatenate(weights, axis=0))
        sums = dot(hi, values) + dot(lo, values)
        col = iota((SRC * IPB, width), 1)
        picked = sums[0 : SRC * IPB]
        for h in range(1, width // HEAD):
            picked = jnp.where(
                col >= h * HEAD, sums[h * SRC * IPB : (h + 1) * SRC * IPB], picked
            )
        pooled[...] += picked

    pass_on(0)

    def slot(s, carry):
        @pl.when(s + 1 < SRC)
        def _():
            pass_on(s + 1)

        got(s, 3, rows.at[s, far, pl.ds(0, mid)]).wait_recv()
        got(s, 4, rows.at[s, far, pl.ds(mid, mid)]).wait_recv()
        share(s, far, 7).start()
        for k, offset in ((2, chip), (5, left // 2), (6, right // 2), (7, far // 2)):
            got(s, k, rows.at[s, offset * 2 + 1 - core]).wait_recv()
        attend(s)
        return carry

    lax.fori_loop(0, SRC, slot, 0)

    r = iota((SRC * IPB, 1), 0)
    label = jnp.zeros((SRC * IPB, 1), jnp.int32)
    place = jnp.zeros((SRC * IPB, 1), jnp.int32)
    count = jnp.ones((SRC * IPB, 1), jnp.int32)
    for s in range(SRC):
        for n in range(IPB):
            here = r == s * IPB + n
            label = jnp.where(here, caption_ref[s, n], label)
            place = jnp.where(here, dest_ref[s] * IPB + n, place)
            count = jnp.where(here, sizes_ref[s, n], count)
    embeds = (pooled[...] * (1.0 / count.astype(F32))).astype(BF16)
    squares = jnp.sum(embeds.astype(F32) * embeds.astype(F32), axis=1, keepdims=True)
    sq0 = squares.astype(BF16).astype(F32)
    sq1 = (squares - sq0).astype(BF16).astype(F32)
    sq2 = squares - sq0 - sq1
    col = iota((SRC * IPB, 256), 1)
    extended = jnp.zeros((SRC * IPB, 256), F32)
    for at, value in (
        (LABEL_HI, (label // 8).astype(F32)),
        (LABEL_LO, (label % 8).astype(F32)),
        (PLACE, place.astype(F32)),
        (SQ0, sq0),
        (SQ1, sq1),
        (SQ2, sq2),
    ):
        extended = jnp.where(col == at, value, extended)
    pack_rows[p] = extended.astype(BF16)
    pack_rows[p, :, 0:width] = embeds

    def embed_copy(d):
        return remote(
            pack_rows.at[p], pack_rows.at[p], e_send.at[d], e_recv.at[p], {"pack": (p + d) % n_pack}
        )

    for d in range(1, n_pack):
        embed_copy(d).start()

    for d in range(1, n_dp):
        src = (g + d) % n_dp
        remote(
            text_rows.at[src], text_rows.at[src], t_send.at[d], t_recv.at[src], {"dp": src}
        ).wait_recv()
    n_texts = n_dp * text_rows.shape[1]
    text_all = text_rows[...].reshape(n_texts, 256)
    text_all = jnp.where(iota((n_texts, 256), 1) < width, text_all, 0.0)
    text_squares = jnp.sum(text_all * text_all, axis=1, keepdims=True)
    text_bf = text_all.astype(BF16)
    pick = iota((16, 256), 1)
    is_square = (pick >= SQ0) & (pick <= SQ2)
    low = iota((16, 256), 0) < 8
    reads = jnp.where(low & is_square, 1.0, 0.0)
    reads = jnp.where(jnp.logical_not(low) & (pick == LABEL_HI), 8.0, reads)
    reads = jnp.where(jnp.logical_not(low) & (pick == LABEL_LO), 1.0, reads)
    left_side = jnp.concatenate([text_bf, reads.astype(BF16)], axis=0)

    for d in range(1, n_pack):
        src = (p + d) % n_pack
        remote(
            pack_rows.at[src], pack_rows.at[src], e_send.at[d], e_recv.at[src], {"pack": src}
        ).wait_recv()

    n_slots = n_pack * SRC * IPB
    n_images = n_pack * DEST * IPB
    loose = pack_rows[...].reshape(n_slots, 256)
    find = jnp.where(iota((128, 256), 1) == PLACE, 1.0, 0.0).astype(BF16)
    placing = dot_t(find, loose) == iota((128, n_slots), 0).astype(F32)
    packed = dot(jnp.where(placing, 1.0, 0.0).astype(BF16), loose).astype(BF16)

    products = dot_t(left_side, packed)
    image_lane = iota((n_texts, 128), 1)
    sims[m, 0:n_texts, :] = jnp.where(image_lane < n_images, products[0:n_texts], text_squares)
    sims[m, n_texts : n_texts + 8, :] = products[n_texts : n_texts + 8]
    labels = products[n_texts + 8 : n_texts + 9]

    def sims_copy(d):
        return remote(sims.at[m], sims.at[m], s_send.at[d], s_recv.at[m], {"mp": (m + d) % n_mp})

    for d in range(1, n_mp):
        sims_copy(d).start()
    text_row = iota((n_texts, 128), 0)
    matching = labels == (((text_row // 8) * n_pack + p) * 8 + text_row % 8).astype(F32)
    sign = jnp.where(matching, 1.0, -1.0)
    for d in range(1, n_mp):
        src = (m + d) % n_mp
        remote(sims.at[src], sims.at[src], s_send.at[d], s_recv.at[src], {"mp": src}).wait_recv()
    total = sims[0]
    for k in range(1, n_mp):
        total = total + sims[k]
    cosine = total[0:n_texts]
    image_scale = lax.rsqrt(total[n_texts : n_texts + 1] + 1e-06)
    text_scale = lax.rsqrt(
        jnp.sum(jnp.where(image_lane == n_images, cosine, 0.0), axis=1, keepdims=True) + 1e-06
    )
    heat = heat_ref[0]
    logits = heat * cosine * image_scale * text_scale + shift_ref[0]
    slopes = -sign * jax.nn.sigmoid(-sign * logits) * heat
    slopes = jnp.where(image_lane < n_images, slopes, 0.0)

    hi, lo = split2(slopes * text_scale)
    contract0 = (((0,), (0,)), ((), ()))
    image_part = lax.dot_general(hi, text_bf, contract0, preferred_element_type=F32)
    image_part += lax.dot_general(lo, text_bf, contract0, preferred_element_type=F32)
    own_image[...] = image_part[0:n_images].reshape(n_pack, 8, 256)

    def image_copy(d):
        to = (p + d) % n_pack
        return remote(
            own_image.at[to], image_terms.at[p], iz_send.at[d], iz_recv.at[p], {"pack": to}
        )

    for d in range(1, n_pack):
        image_copy(d).start()

    hi, lo = split2(slopes * jnp.where(iota((1, 128), 1) < n_images, image_scale, 0.0))
    text_part = dot(hi, packed) + dot(lo, packed)
    own_text[...] = text_part.reshape(n_dp, 8, 256)

    def text_term_copy(d):
        to = (g + d) % n_dp
        return remote(own_text.at[to], text_terms.at[g], ty_send.at[d], ty_recv.at[g], {"dp": to})

    for d in range(1, n_dp):
        text_term_copy(d).start()

    image_terms[p] = own_image[p]
    text_terms[g] = own_text[g]
    for d in range(1, n_dp):
        src = (g + d) % n_dp
        remote(
            own_text.at[src], text_terms.at[src], ty_send.at[d], ty_recv.at[src], {"dp": src}
        ).wait_recv()
    text_out[...] = jnp.sum(text_terms[...], axis=0)[:, 0:width]
    for d in range(1, n_pack):
        src = (p + d) % n_pack
        remote(
            own_image.at[src], image_terms.at[src], iz_send.at[d], iz_recv.at[src], {"pack": src}
        ).wait_recv()
    image_out[...] = jnp.sum(image_terms[...], axis=0)[:, 0:width]

    def sent(s, carry):
        own_to_right(s).wait_send()
        own_to_left(s).wait_send()
        own_to_twin(s).wait_send()
        pass_right(s).wait_send()
        pass_left(s).wait_send()
        share(s, left, 5).wait_send()
        share(s, right, 6).wait_send()
        share(s, far, 7).wait_send()
        return carry

    lax.fori_loop(0, SRC, sent, 0)
    for d in range(1, n_dp):
        text_copy(d).wait_send()
        text_term_copy(d).wait_send()
    for d in range(1, n_pack):
        embed_copy(d).wait_send()
        image_copy(d).wait_send()
    for d in range(1, n_mp):
        sims_copy(d).wait_send()


def on_device(
    n_dp,
    n_pack,
    n_mp,
    tile_activity,
    tokens_per_picture,
    slot_destinations,
    caption_indices,
    attention_projections,
    caption_vectors,
    score_inverse_heat,
    score_shift,
):
    width = caption_vectors.shape[1]
    depth = attention_projections.shape[1]
    n_texts = n_dp * caption_vectors.shape[0]
    vmem = pl.BlockSpec(memory_space=pltpu.VMEM)
    smem = pl.BlockSpec(memory_space=pltpu.SMEM)
    hbm = pl.BlockSpec(memory_space=pl.ANY)
    dma = pltpu.SemaphoreType.DMA
    return pl.pallas_call(
        functools.partial(kernel, n_dp, n_pack, n_mp),
        out_shape=(
            jax.ShapeDtypeStruct(caption_vectors.shape, F32),
            jax.ShapeDtypeStruct(caption_vectors.shape, F32),
        ),
        in_specs=[hbm, smem, smem, smem, hbm, vmem, smem, smem],
        out_specs=(vmem, vmem),
        scratch_shapes=[
            pltpu.VMEM((SRC, BLK, width), BF16),
            pltpu.VMEM((3, depth, width), BF16),
            pltpu.VMEM((SRC, n_mp, BLK + BLK // 2, 128), BF16),
            pltpu.VMEM((3, n_mp * 128, width), BF16),
            pltpu.VMEM((3, n_mp * 128, width), BF16),
            pltpu.VMEM((3, n_mp * 128, width), BF16),
            pltpu.VMEM((BLK, 256), BF16),
            pltpu.VMEM((BLK, 256), BF16),
            pltpu.VMEM((SRC * IPB, width), F32),
            pltpu.VMEM((n_dp, 8, 256), F32),
            pltpu.VMEM((n_pack, SRC * IPB, 256), BF16),
            pltpu.VMEM((n_mp, n_texts + 8, 128), F32),
            pltpu.VMEM((n_dp, 8, 256), F32),
            pltpu.VMEM((n_pack, 8, 256), F32),
            pltpu.VMEM((n_dp, 8, 256), F32),
            pltpu.VMEM((n_pack, 8, 256), F32),
            dma((2,)),
            dma((SRC, 8)),
            dma((SRC, 8)),
            dma((n_dp,)),
            dma((n_dp,)),
            dma((n_pack,)),
            dma((n_pack,)),
            dma((n_mp,)),
            dma((n_mp,)),
            dma((n_dp,)),
            dma((n_dp,)),
            dma((n_pack,)),
            dma((n_pack,)),
        ],
        compiler_params=pltpu.CompilerParams(
            collective_id=0, has_side_effects=True, vmem_limit_bytes=40 * 1024 * 1024
        ),
        name="contrastive_step",
    )(
        tile_activity,
        tokens_per_picture,
        slot_destinations,
        caption_indices,
        attention_projections,
        caption_vectors,
        score_inverse_heat,
        score_shift,
    )


def solution(mesh):
    sizes = (mesh.shape["dp"], mesh.shape["pack"], mesh.shape["mp"])
    return jax.shard_map(
        functools.partial(on_device, *sizes),
        mesh=mesh,
        in_specs=(
            P(("dp", "pack"), None, "mp"),
            P(("dp", "pack"), None),
            P(("dp", "pack")),
            P(("dp", "pack"), None),
            P(None, None, "mp"),
            P(("dp", "pack"), "mp"),
            P(),
            P(),
        ),
        out_specs=(P(("dp", "pack"), "mp"), P(("dp", "pack"), "mp")),
        check_vma=False,
    )
```

time: 870 us -> 74.1 us (0.09)
  waiting for transfers between devices: 712 us -> 0 us
  blocking collectives: 118 us -> 0 us
  Pallas kernels: 0 us -> 66.7 us
  matrix products: 15.5 us -> 0 us
  between operations: 15.1 us -> 2.01 us
    reduce_scatter x1 -> x0, waiting for transfers between devices: 662 us -> none  [on_device(): lax.psum_scatter(partial_grads, ('dp', 'pack'), scatter_dimension=0, tile...]
    all_gather x2 -> x0, blocking collectives: 82 us -> none  [the longest x1 54.3 us: on_device(): lax.all_gather(caption_vectors, ('dp', 'pack'), axis=0, tiled=True)]
    pallas_call x0 -> x1, Pallas kernels: none -> 66.7 us  [on_device(): pl.pallas_call(functools.partial(kernel, n_dp, n_pack, n_mp), out_shape=(...]
    all_gather x2 -> x0, waiting for transfers between devices: 49.2 us -> none  [the longest x1 49.1 us: on_device(): lax.all_gather(tile_activity, 'pack', axis=0, tiled=True)]
    psum x1 -> x0, blocking collectives: 36.3 us -> none  [on_device(): lax.psum((similarity_products, own_squares, text_squares), 'mp')]
    dot_general x6 -> x0, matrix products: 11.2 us -> none  [the longest x1 5.68 us: on_device(): jnp.einsum('sb,bpf->spf', placing.astype(jnp.bfloat16), arrived, preferre...]
  transfers between devices with their start and end apart: 3 -> 0, of which waited for: 2 -> 0; matrix products, arithmetic and copies ran while one was open for 0% -> 0% of each run, Pallas kernels for 0% -> 0%
where the time goes in v1:
time: 74.1 us; the launch traced here: 73.9 us
  Pallas kernels  66.7 us (90%)
  local copies, waits for them, and re-layouts  5.13 us (7%)
  between operations  2.01 us (3%)
    pallas_call x1, Pallas kernels, on_device(): pl.pallas_call(functools.partial(kernel, n_dp, n_pack, n_mp), out_shape=(...  66.7 us
    unnamed x12, local copies, waits for them, and re-layouts  5.13 us

profile of v1, /device:TPU:1, one launch (start us, length us, event | category | flops | bytes accessed | tf_op | source)
XLA Modules:
  0.0 73.9 jit_solution(163781431063538085)
XLA Ops:
  1.9 0.0 copy-start
  1.9 0.0 copy-start.1
  1.9 0.0 copy-start.2
  2.0 0.0 copy-start.3
  2.0 1.2 %copy.10.tile_hbm = bf16[4,256,192]{2,1,0:T(8,128)(2,1)S(1)} copy(bf16[4,256,192]{1,2,0:T(8,128)(2,1)} %param.8) | data formatting | bytes 786432 | tf_op args[0]
  3.2 2.7 %copy.11.proj_hbm = bf16[3,1536,192]{2,1,0:T(8,128)(2,1)S(1)} copy(bf16[3,1536,192]{1,2,0:T(8,128)(2,1)} %param.12) | data formatting | bytes 3538944 | tf_op args[4]
  5.9 0.0 copy-done
  5.9 0.0 copy-done.1
  5.9 0.0 copy-done.2
  5.9 0.0 copy-done.3
  5.9 66.7 %contrastive_step.1 = (f32[8,192]{1,0:T(8,128)S(1)}, f32[8,192]{1,0:T(8,128)S(1)}) custom-call(bf16[4,256,192]{2,1,0:T(8,128)(2,1)S(1)} %copy.10.tile_hbm, s32[4,4]{1,0:T(4,128)S(1)} %copy-done.1, s32[4]{0:T(128)S(1)} %copy-done.3, s32[4,4]{1,0:T(4,128)S(1)} %copy-done.2, bf16[3,1536,192]{2,1,0:T(8,128)(2,1)S(1)} %copy.11.proj_hbm, ...), custom_call_target="tpu_custom_call" | custom-call | tf_op jit(solution)/shard_map/contrastive_step/pallas_call | solution.py:439
  72.7 0.6 copy.16
  73.3 0.6 copy.17
Async XLA Ops:
  1.9 4.0 %copy-start = (bf16[8,192]{1,0:T(8,128)(2,1)S(1)}, bf16[8,192]{1,0:T(8,128)(2,1)}, u32[]{:S(2)}) copy-start(bf16[8,192]{1,0:T(8,128)(2,1)} %texts_ref.1) | copy-start | bytes 9220
  1.9 4.0 %copy-start.1 = (s32[4,4]{1,0:T(4,128)S(1)}, s32[4,4]{1,0:T(4,128)}, u32[]{:S(2)}) copy-start(s32[4,4]{1,0:T(4,128)} %sizes_ref.1) | copy-start | bytes 196
  1.9 4.0 %copy-start.2 = (s32[4,4]{1,0:T(4,128)S(1)}, s32[4,4]{1,0:T(4,128)}, u32[]{:S(2)}) copy-start(s32[4,4]{1,0:T(4,128)} %caption_ref.1) | copy-start | bytes 196
  2.0 4.0 %copy-start.3 = (s32[4]{0:T(128)S(1)}, s32[4]{0:T(128)}, u32[]{:S(2)}) copy-start(s32[4]{0:T(128)} %dest_ref.1) | copy-start | bytes 52

commit v2 on v1

--- a/solution.py
+++ b/solution.py
@@ -36,32 +36,32 @@
     return hi, (a - hi.astype(F32)).astype(BF16)
 
 
+def far_first(n):
+    return sorted(range(1, n), key=lambda d: -min(d, n - d))
+
+
 def kernel(
     n_dp,
     n_pack,
     n_mp,
     tile_hbm,
-    sizes_ref,
-    dest_ref,
-    caption_ref,
+    info_hbm,
     proj_hbm,
     texts_ref,
+    heat_hbm,
+    shift_hbm,
+    image_out,
+    text_out,
+    info_ref,
     heat_ref,
     shift_ref,
-    image_out,
-    text_out,
-    raw,
     proj,
     rows,
-    w_main,
-    w_low,
-    w_high,
-    qx,
-    kx,
     pooled,
     text_rows,
     pack_rows,
     sims,
+    halves,
     own_text,
     own_image,
     text_terms,
@@ -89,10 +89,22 @@
     twin = chip * 2 + 1 - core
     width = texts_ref.shape[1]
 
-    load_tile = pltpu.make_async_copy(tile_hbm, raw, load_sem.at[0])
+    load_tile = pltpu.make_async_copy(tile_hbm, rows.at[:, m], load_sem.at[0])
     load_proj = pltpu.make_async_copy(proj_hbm, proj, load_sem.at[1])
     load_tile.start()
     load_proj.start()
+    scalars = [
+        pltpu.make_async_copy(src, dst, load_sem.at[2 + i])
+        for i, (src, dst) in enumerate(
+            (
+                (info_hbm, info_ref),
+                (heat_hbm, heat_ref),
+                (shift_hbm, shift_ref),
+            )
+        )
+    ]
+    for copy in scalars:
+        copy.start()
 
     barrier = pltpu.get_barrier_semaphore()
     for d in range(1, n_mp):
@@ -104,14 +116,6 @@
             barrier, inc=1, device_id={"pack": (p + d) % n_pack}, device_id_type=MESH
         )
 
-    load_tile.wait()
-    half = BLK // 2
-    for s in range(SRC):
-        rows[s, m, 0:BLK, :] = raw[s, :, 0:128]
-        tail = jnp.concatenate(
-            [raw[s, 0:half, 128:192].astype(F32), raw[s, half:BLK, 128:192].astype(F32)], axis=1
-        )
-        rows[s, m, BLK : BLK + half, :] = tail.astype(BF16)
     text_rows[g] = jnp.zeros((8, 256), F32)
     text_rows[g, :, 0:width] = texts_ref[...].astype(F32)
 
@@ -127,24 +131,27 @@
             device_id_type=MESH,
         )
 
-    mid = (BLK + half) // 2
-
     def own_to_right(s):
-        return remote(rows.at[s, m], rows.at[s, m], x_send.at[s, 0], x_recv.at[s, 0], {"mp": right})
+        return remote(tile_hbm.at[s], rows.at[s, m], x_send.at[s, 0], x_recv.at[s, 0], {"mp": right})
 
     def own_to_left(s):
-        return remote(rows.at[s, m], rows.at[s, m], x_send.at[s, 1], x_recv.at[s, 1], {"mp": left})
+        return remote(tile_hbm.at[s], rows.at[s, m], x_send.at[s, 1], x_recv.at[s, 1], {"mp": left})
 
     def own_to_twin(s):
-        return remote(rows.at[s, m], rows.at[s, m], x_send.at[s, 2], x_recv.at[s, 2], {"mp": twin})
+        return remote(tile_hbm.at[s], rows.at[s, m], x_send.at[s, 2], x_recv.at[s, 2], {"mp": twin})
+
+    def own_to_far(s):
+        return remote(tile_hbm.at[s], rows.at[s, m], x_send.at[s, 3], x_recv.at[s, 3], {"mp": far})
+
+    mid = width // 2
 
     def pass_right(s):
         part = rows.at[s, left, pl.ds(0, mid)]
-        return remote(part, part, x_send.at[s, 3], x_recv.at[s, 3], {"mp": right})
+        return remote(part, part, x_send.at[s, 6], x_recv.at[s, 6], {"mp": right})
 
     def pass_left(s):
         part = rows.at[s, right, pl.ds(mid, mid)]
-        return remote(part, part, x_send.at[s, 4], x_recv.at[s, 4], {"mp": left})
+        return remote(part, part, x_send.at[s, 8], x_recv.at[s, 8], {"mp": left})
 
     def share(s, whose, k):
         part = rows.at[s, whose]
@@ -153,44 +160,43 @@
     def got(s, k, part):
         return remote(part, part, x_send.at[s, k], x_recv.at[s, k], {"mp": twin})
 
-    for s in range(SRC):
+    def send_near(s):
         own_to_right(s).start()
         own_to_left(s).start()
         own_to_twin(s).start()
+
+    def take_near(s, hand_on):
+        got(s, 0, rows.at[s, left]).wait_recv()
+        if hand_on:
+            pass_right(s).start()
+        share(s, left, 4).start()
+        got(s, 1, rows.at[s, right]).wait_recv()
+        if hand_on:
+            pass_left(s).start()
+        share(s, right, 5).start()
+
+    last = SRC - 1
+    send_near(0)
+    send_near(1)
 
     def text_copy(d):
         return remote(
             text_rows.at[g], text_rows.at[g], t_send.at[d], t_recv.at[g], {"dp": (g + d) % n_dp}
         )
 
-    for d in range(1, n_dp):
+    for d in far_first(n_dp):
         text_copy(d).start()
 
     load_proj.wait()
-    w_low[...] = jnp.zeros_like(w_low)
-    w_high[...] = jnp.zeros_like(w_high)
-    for c in range(3):
-        for k in range(n_mp):
-            w_main[c, k * 128 : k * 128 + 128, :] = proj[c, k * width : k * width + 128, :]
-            rest = proj[c, k * width + 128 : k * width + 192, :]
-            w_low[c, k * 128 : k * 128 + 64, :] = rest
-            w_high[c, k * 128 + 64 : k * 128 + 128, :] = rest
+    load_tile.wait()
+    for copy in scalars:
+        copy.wait()
     pooled[...] = jnp.zeros_like(pooled)
 
-    def pass_on(s):
-        got(s, 0, rows.at[s, left]).wait_recv()
-        pass_right(s).start()
-        share(s, left, 5).start()
-        got(s, 1, rows.at[s, right]).wait_recv()
-        pass_left(s).start()
-        share(s, right, 6).start()
-
-    lane = iota((BLK, 256), 1)
-
     def attend(s):
-        e1 = sizes_ref[s, 0]
-        e2 = e1 + sizes_ref[s, 1]
-        e3 = e2 + sizes_ref[s, 2]
+        e1 = info_ref[s, 1]
+        e2 = e1 + info_ref[s, 2]
+        e3 = e2 + info_ref[s, 3]
 
         def image_of(position):
             return (
@@ -199,37 +205,34 @@
                 + (position >= e3).astype(jnp.int32)
             )
 
-        same = image_of(iota((BLK, 256), 0)) == lane - width
-        extra = (lane >= width) & (lane < width + IPB)
-        qx[...] = jnp.where(extra & same, -1e30, 0.0).astype(BF16)
-        kx[...] = jnp.where(extra & jnp.logical_not(same), 1.0, 0.0).astype(BF16)
-
-        main = jnp.concatenate([rows[s, k, 0:BLK, :] for k in range(n_mp)], axis=1)
-        tails = jnp.concatenate([rows[s, k, BLK : BLK + half, :] for k in range(n_mp)], axis=1)
-
-        def project(c):
-            return dot(main, w_main[c]) + jnp.concatenate(
-                [dot(tails, w_low[c]), dot(tails, w_high[c])], axis=0
-            )
-
-        qx[:, 0:width] = (project(0) * HEAD**-0.5).astype(BF16)
-        kx[:, 0:width] = project(1).astype(BF16)
-        values = project(2).astype(BF16)
-        keys = kx[...]
-        queries = qx[...]
+        image = iota((16, BLK), 0)
+        same = image_of(iota((16, BLK), 1)) == image
+        query_extra = jnp.where((image < IPB) & same, -1e30, 0.0).astype(BF16)
+        key_extra = jnp.where((image < IPB) & jnp.logical_not(same), 1.0, 0.0).astype(BF16)
+
+        features = rows[s].reshape(n_mp * width, BLK)
+        projected = dot(proj[...].reshape(3 * width, n_mp * width), features)
+        queries = (projected[0:width] * HEAD**-0.5).astype(BF16)
+        keys = projected[width : 2 * width].astype(BF16)
+        values = projected[2 * width : 3 * width].astype(BF16)
 
         row16 = iota((SRC * IPB, BLK), 0)
         member = (row16 // IPB == s) & (row16 % IPB == image_of(iota((SRC * IPB, BLK), 1)))
         member = jnp.where(member, 1.0, 0.0).astype(BF16)
         weights = []
         for h in range(width // HEAD):
-            keep = ((lane >= h * HEAD) & (lane < (h + 1) * HEAD)) | (lane >= width)
-            scores = dot_t(keys, jnp.where(keep, queries, jnp.zeros_like(queries)))
+            head = slice(h * HEAD, (h + 1) * HEAD)
+            scores = lax.dot_general(
+                jnp.concatenate([keys[head], key_extra], axis=0),
+                jnp.concatenate([queries[head], query_extra], axis=0),
+                (((0,), (0,)), ((), ())),
+                preferred_element_type=F32,
+            )
             exponent = jnp.exp(scores - jnp.max(scores, axis=0, keepdims=True))
             inverse = 1.0 / jnp.sum(exponent, axis=0, keepdims=True)
             weights.append(dot_t(member, (exponent * inverse).astype(BF16)))
         hi, lo = split2(jnp.concatenate(weights, axis=0))
-        sums = dot(hi, values) + dot(lo, values)
+        sums = dot_t(hi, values) + dot_t(lo, values)
         col = iota((SRC * IPB, width), 1)
         picked = sums[0 : SRC * IPB]
         for h in range(1, width // HEAD):
@@ -238,17 +241,32 @@
             )
         pooled[...] += picked
 
-    pass_on(0)
+    take_near(0, True)
+    send_near(2)
+    take_near(1, True)
+    send_near(3)
 
     def slot(s, carry):
-        @pl.when(s + 1 < SRC)
+        @pl.when(s == 1)
         def _():
-            pass_on(s + 1)
-
-        got(s, 3, rows.at[s, far, pl.ds(0, mid)]).wait_recv()
-        got(s, 4, rows.at[s, far, pl.ds(mid, mid)]).wait_recv()
+            take_near(2, True)
+            own_to_far(last).start()
+
+        @pl.when(s == 2)
+        def _():
+            take_near(last, False)
+
+        @pl.when(s < last)
+        def _():
+            got(s, 6, rows.at[s, far, pl.ds(0, mid)]).wait_recv()
+            got(s, 8, rows.at[s, far, pl.ds(mid, mid)]).wait_recv()
+
+        @pl.when(s == last)
+        def _():
+            got(s, 3, rows.at[s, far]).wait_recv()
+
         share(s, far, 7).start()
-        for k, offset in ((2, chip), (5, left // 2), (6, right // 2), (7, far // 2)):
+        for k, offset in ((2, chip), (4, left // 2), (5, right // 2), (7, far // 2)):
             got(s, k, rows.at[s, offset * 2 + 1 - core]).wait_recv()
         attend(s)
         return carry
@@ -262,9 +280,9 @@
     for s in range(SRC):
         for n in range(IPB):
             here = r == s * IPB + n
-            label = jnp.where(here, caption_ref[s, n], label)
-            place = jnp.where(here, dest_ref[s] * IPB + n, place)
-            count = jnp.where(here, sizes_ref[s, n], count)
+            label = jnp.where(here, info_ref[s, 1 + IPB + n], label)
+            place = jnp.where(here, info_ref[s, 0] * IPB + n, place)
+            count = jnp.where(here, info_ref[s, 1 + n], count)
     embeds = (pooled[...] * (1.0 / count.astype(F32))).astype(BF16)
     squares = jnp.sum(embeds.astype(F32) * embeds.astype(F32), axis=1, keepdims=True)
     sq0 = squares.astype(BF16).astype(F32)
@@ -289,7 +307,7 @@
             pack_rows.at[p], pack_rows.at[p], e_send.at[d], e_recv.at[p], {"pack": (p + d) % n_pack}
         )
 
-    for d in range(1, n_pack):
+    for d in far_first(n_pack):
         embed_copy(d).start()
 
     for d in range(1, n_dp):
@@ -329,20 +347,24 @@
     sims[m, n_texts : n_texts + 8, :] = products[n_texts : n_texts + 8]
     labels = products[n_texts + 8 : n_texts + 9]
 
-    def sims_copy(d):
-        return remote(sims.at[m], sims.at[m], s_send.at[d], s_recv.at[m], {"mp": (m + d) % n_mp})
-
-    for d in range(1, n_mp):
-        sims_copy(d).start()
+    def sims_copy(k):
+        to = (far, right, left)[k]
+        return remote(sims.at[m], sims.at[m], s_send.at[k], s_recv.at[k], {"mp": to})
+
+    for k in range(3):
+        sims_copy(k).start()
     text_row = iota((n_texts, 128), 0)
     matching = labels == (((text_row // 8) * n_pack + p) * 8 + text_row % 8).astype(F32)
     sign = jnp.where(matching, 1.0, -1.0)
-    for d in range(1, n_mp):
-        src = (m + d) % n_mp
-        remote(sims.at[src], sims.at[src], s_send.at[d], s_recv.at[src], {"mp": src}).wait_recv()
-    total = sims[0]
-    for k in range(1, n_mp):
-        total = total + sims[k]
+    for k, src in enumerate((far, left, right)):
+        remote(sims.at[src], sims.at[src], s_send.at[k], s_recv.at[k], {"mp": src}).wait_recv()
+    halves[core] = (sims[core] + sims[2 + core]) + (sims[4 + core] + sims[6 + core])
+    half_copy = remote(
+        halves.at[core], halves.at[core], s_send.at[3], s_recv.at[3], {"mp": twin}
+    )
+    half_copy.start()
+    half_copy.wait_recv()
+    total = halves[0] + halves[1]
     cosine = total[0:n_texts]
     image_scale = lax.rsqrt(total[n_texts : n_texts + 1] + 1e-06)
     text_scale = lax.rsqrt(
@@ -365,7 +387,7 @@
             own_image.at[to], image_terms.at[p], iz_send.at[d], iz_recv.at[p], {"pack": to}
         )
 
-    for d in range(1, n_pack):
+    for d in far_first(n_pack):
         image_copy(d).start()
 
     hi, lo = split2(slopes * jnp.where(iota((1, 128), 1) < n_images, image_scale, 0.0))
@@ -376,7 +398,7 @@
         to = (g + d) % n_dp
         return remote(own_text.at[to], text_terms.at[g], ty_send.at[d], ty_recv.at[g], {"dp": to})
 
-    for d in range(1, n_dp):
+    for d in far_first(n_dp):
         text_term_copy(d).start()
 
     image_terms[p] = own_image[p]
@@ -394,26 +416,27 @@
         ).wait_recv()
     image_out[...] = jnp.sum(image_terms[...], axis=0)[:, 0:width]
 
-    def sent(s, carry):
+    for s in range(SRC):
         own_to_right(s).wait_send()
         own_to_left(s).wait_send()
         own_to_twin(s).wait_send()
-        pass_right(s).wait_send()
-        pass_left(s).wait_send()
-        share(s, left, 5).wait_send()
-        share(s, right, 6).wait_send()
+        share(s, left, 4).wait_send()
+        share(s, right, 5).wait_send()
         share(s, far, 7).wait_send()
-        return carry
-
-    lax.fori_loop(0, SRC, sent, 0)
+        if s < last:
+            pass_right(s).wait_send()
+            pass_left(s).wait_send()
+        else:
+            own_to_far(s).wait_send()
     for d in range(1, n_dp):
         text_copy(d).wait_send()
         text_term_copy(d).wait_send()
     for d in range(1, n_pack):
         embed_copy(d).wait_send()
         image_copy(d).wait_send()
-    for d in range(1, n_mp):
-        sims_copy(d).wait_send()
+    for k in range(3):
+        sims_copy(k).wait_send()
+    half_copy.wait_send()
 
 
 def on_device(
@@ -432,9 +455,11 @@
     width = caption_vectors.shape[1]
     depth = attention_projections.shape[1]
     n_texts = n_dp * caption_vectors.shape[0]
+    block_info = jnp.concatenate(
+        [slot_destinations[:, None], tokens_per_picture, caption_indices], axis=1
+    )
     vmem = pl.BlockSpec(memory_space=pltpu.VMEM)
-    smem = pl.BlockSpec(memory_space=pltpu.SMEM)
-    hbm = pl.BlockSpec(memory_space=pl.ANY)
+    hbm = pl.BlockSpec(memory_space=pltpu.HBM)
     dma = pltpu.SemaphoreType.DMA
     return pl.pallas_call(
         functools.partial(kernel, n_dp, n_pack, n_mp),
@@ -442,49 +467,45 @@
             jax.ShapeDtypeStruct(caption_vectors.shape, F32),
             jax.ShapeDtypeStruct(caption_vectors.shape, F32),
         ),
-        in_specs=[hbm, smem, smem, smem, hbm, vmem, smem, smem],
+        in_specs=[hbm, hbm, hbm, vmem, hbm, hbm],
         out_specs=(vmem, vmem),
         scratch_shapes=[
-            pltpu.VMEM((SRC, BLK, width), BF16),
-            pltpu.VMEM((3, depth, width), BF16),
-            pltpu.VMEM((SRC, n_mp, BLK + BLK // 2, 128), BF16),
-            pltpu.VMEM((3, n_mp * 128, width), BF16),
-            pltpu.VMEM((3, n_mp * 128, width), BF16),
-            pltpu.VMEM((3, n_mp * 128, width), BF16),
-            pltpu.VMEM((BLK, 256), BF16),
-            pltpu.VMEM((BLK, 256), BF16),
+            pltpu.SMEM(block_info.shape, jnp.int32),
+            pltpu.SMEM((1,), F32),
+            pltpu.SMEM((1,), F32),
+            pltpu.VMEM((3, width, depth), BF16),
+            pltpu.VMEM((SRC, n_mp, width, BLK), BF16),
             pltpu.VMEM((SRC * IPB, width), F32),
             pltpu.VMEM((n_dp, 8, 256), F32),
             pltpu.VMEM((n_pack, SRC * IPB, 256), BF16),
             pltpu.VMEM((n_mp, n_texts + 8, 128), F32),
+            pltpu.VMEM((2, n_texts + 8, 128), F32),
             pltpu.VMEM((n_dp, 8, 256), F32),
             pltpu.VMEM((n_pack, 8, 256), F32),
             pltpu.VMEM((n_dp, 8, 256), F32),
             pltpu.VMEM((n_pack, 8, 256), F32),
-            dma((2,)),
-            dma((SRC, 8)),
-            dma((SRC, 8)),
+            dma((5,)),
+            dma((SRC, 9)),
+            dma((SRC, 9)),
             dma((n_dp,)),
             dma((n_dp,)),
             dma((n_pack,)),
             dma((n_pack,)),
-            dma((n_mp,)),
-            dma((n_mp,)),
+            dma((4,)),
+            dma((4,)),
             dma((n_dp,)),
             dma((n_dp,)),
             dma((n_pack,)),
             dma((n_pack,)),
         ],
         compiler_params=pltpu.CompilerParams(
-            collective_id=0, has_side_effects=True, vmem_limit_bytes=40 * 1024 * 1024
+            collective_id=0, has_side_effects=True, vmem_limit_bytes=55040 * 1024
         ),
         name="contrastive_step",
     )(
-        tile_activity,
-        tokens_per_picture,
-        slot_destinations,
-        caption_indices,
-        attention_projections,
+        jnp.swapaxes(tile_activity, 1, 2),
+        block_info,
+        jnp.swapaxes(attention_projections, 1, 2),
         caption_vectors,
         score_inverse_heat,
         score_shift,

time: 74.1 us -> 66.9 us (0.903)
  Pallas kernels: 66.7 us -> 61.3 us
  local copies, waits for them, and re-layouts: 5.13 us -> 2.63 us
  other arithmetic: 0 us -> 0.77 us
    pallas_call x1, Pallas kernels: 66.7 us -> 61.3 us  [on_device(): pl.pallas_call(functools.partial(kernel, n_dp, n_pack, n_mp), out_shape=(...]
    unnamed x12 -> x4, local copies, waits for them, and re-layouts: 5.13 us -> 1.89 us
    concatenate x0 -> x1, other arithmetic: none -> 0.77 us  [on_device(): jnp.concatenate([slot_destinations[:, None], tokens_per_picture, caption_...]
    broadcast_in_dim x0 -> x1, local copies, waits for them, and re-layouts: none -> 0.74 us  [on_device(): slot_destinations[:, None]]
where the time goes in v2:
time: 66.9 us; the launch traced here: 66.7 us
  Pallas kernels  61.3 us (92%)
  local copies, waits for them, and re-layouts  2.63 us (4%)
  between operations  1.93 us (3%)
  other arithmetic  0.77 us (1%)
    pallas_call x1, Pallas kernels, on_device(): pl.pallas_call(functools.partial(kernel, n_dp, n_pack, n_mp), out_shape=(...  61.3 us
    unnamed x4, local copies, waits for them, and re-layouts  1.89 us

profile of v2, /device:TPU:1, one launch (start us, length us, event | category | flops | bytes accessed | tf_op | source)
XLA Modules:
  0.0 66.7 jit_solution(8006339402322443035)
XLA Ops:
  1.9 0.7 %copy.10 = s32[4,1]{1,0:T(4,128)S(1)} copy(s32[4,1]{0,1:T(1,128)} %bitcast.5) | data formatting | bytes 32 | tf_op jit(solution)/shard_map/broadcast_in_dim | solution.py:459
  2.7 0.8 %pad_add_fusion.info_hbm = s32[4,9]{1,0:T(4,128)S(1)} fusion(s32[4,4]{1,0:T(4,128)} %param.11, s32[4,4]{1,0:T(4,128)} %param.9, s32[4,1]{1,0:T(4,128)S(1)} %copy.10), kind=kLoop, calls=%fused_computation | loop fusion | flops 72 | bytes 288 | tf_op jit(solution)/shard_map/concatenate | solution.py:458
  3.4 0.0 copy-start
  3.4 0.7 %copy-done = bf16[8,192]{1,0:T(8,128)(2,1)S(1)} copy-done((bf16[8,192]{1,0:T(8,128)(2,1)S(1)}, bf16[8,192]{1,0:T(8,128)(2,1)}, u32[]{:S(2)}) %copy-start) | copy-done | bytes 3096
  4.1 61.3 %contrastive_step.1 = (f32[8,192]{1,0:T(8,128)S(1)}, f32[8,192]{1,0:T(8,128)S(1)}) custom-call(bf16[4,192,256]{2,1,0:T(8,128)(2,1)} %bitcast.4, s32[4,9]{1,0:T(4,128)S(1)} %pad_add_fusion.info_hbm, bf16[3,192,1536]{2,1,0:T(8,128)(2,1)} %bitcast.3, bf16[8,192]{1,0:T(8,128)(2,1)S(1)} %copy-done, f32[1]{0:T(128)S(6)} %copy.13.heat_hbm, f32[1]{0:T(128)S(6)} %copy.14.shift_hbm), custom_call_target="tpu_custom_call" | custom-call | tf_op jit(solution)/shard_map/contrastive_step/pallas_call | solution.py:464
  65.5 0.6 copy.15
  66.1 0.6 copy.16
Async XLA Ops:
  3.4 0.7 %copy-start = (bf16[8,192]{1,0:T(8,128)(2,1)S(1)}, bf16[8,192]{1,0:T(8,128)(2,1)}, u32[]{:S(2)}) copy-start(bf16[8,192]{1,0:T(8,128)(2,1)} %texts_ref.1) | copy-start | bytes 9220

commit v3 on v2

--- a/solution.py
+++ b/solution.py
@@ -60,6 +60,9 @@
     pooled,
     text_rows,
     pack_rows,
+    late_rows,
+    marks,
+    inverse_count,
     sims,
     halves,
     own_text,
@@ -73,6 +76,8 @@
     t_recv,
     e_send,
     e_recv,
+    l_send,
+    l_recv,
     s_send,
     s_recv,
     ty_send,
@@ -193,10 +198,20 @@
         copy.wait()
     pooled[...] = jnp.zeros_like(pooled)
 
-    def attend(s):
-        e1 = info_ref[s, 1]
-        e2 = e1 + info_ref[s, 2]
-        e3 = e2 + info_ref[s, 3]
+    def project(s, whose):
+        weights = [
+            proj[:, :, pl.ds(pl.multiple_of(c * 2 * width, 128), 2 * width)] for c in whose
+        ]
+        features = [rows[s, pl.ds(c * 2, 2)].reshape(2 * width, BLK) for c in whose]
+        return dot(
+            jnp.concatenate(weights, axis=2).reshape(3 * width, len(whose) * 2 * width),
+            jnp.concatenate(features, axis=0),
+        )
+
+    def attend(s, projected):
+        e1 = info_ref[s, 0]
+        e2 = e1 + info_ref[s, 1]
+        e3 = e2 + info_ref[s, 2]
 
         def image_of(position):
             return (
@@ -210,8 +225,6 @@
         query_extra = jnp.where((image < IPB) & same, -1e30, 0.0).astype(BF16)
         key_extra = jnp.where((image < IPB) & jnp.logical_not(same), 1.0, 0.0).astype(BF16)
 
-        features = rows[s].reshape(n_mp * width, BLK)
-        projected = dot(proj[...].reshape(3 * width, n_mp * width), features)
         queries = (projected[0:width] * HEAD**-0.5).astype(BF16)
         keys = projected[width : 2 * width].astype(BF16)
         values = projected[2 * width : 3 * width].astype(BF16)
@@ -233,24 +246,56 @@
             weights.append(dot_t(member, (exponent * inverse).astype(BF16)))
         hi, lo = split2(jnp.concatenate(weights, axis=0))
         sums = dot_t(hi, values) + dot_t(lo, values)
-        col = iota((SRC * IPB, width), 1)
+        out_col = iota((SRC * IPB, width), 1)
         picked = sums[0 : SRC * IPB]
         for h in range(1, width // HEAD):
             picked = jnp.where(
-                col >= h * HEAD, sums[h * SRC * IPB : (h + 1) * SRC * IPB], picked
+                out_col >= h * HEAD, sums[h * SRC * IPB : (h + 1) * SRC * IPB], picked
             )
-        pooled[...] += picked
+        pooled[:, 0:width] += picked
 
     take_near(0, True)
     send_near(2)
     take_near(1, True)
     send_near(3)
+    own_to_far(last).start()
+
+    r = iota((SRC * IPB, 1), 0)
+    label = jnp.zeros((SRC * IPB, 1), jnp.int32)
+    place = jnp.zeros((SRC * IPB, 1), jnp.int32)
+    count = jnp.ones((SRC * IPB, 1), jnp.int32)
+    for k in range(SRC):
+        for n in range(IPB):
+            here = r == k * IPB + n
+            label = jnp.where(here, info_ref[SRC + k, n], label)
+            place = jnp.where(here, info_ref[0, IPB + k] * IPB + n, place)
+            count = jnp.where(here, info_ref[k, n], count)
+    inverse_count[...] = jnp.broadcast_to(1.0 / count.astype(F32), inverse_count.shape)
+    col = iota((SRC * IPB, 256), 1)
+    marks[...] = jnp.zeros_like(marks)
+    for at, value in ((LABEL_HI, label // 8), (LABEL_LO, label % 8), (PLACE, place)):
+        marks[...] = jnp.where(col == at, value.astype(F32), marks[...])
+
+    def image_rows():
+        means = (pooled[...] * inverse_count[...]).astype(BF16).astype(F32)
+        squares = jnp.sum(means * means, axis=1, keepdims=True)
+        sq0 = squares.astype(BF16).astype(F32)
+        sq1 = (squares - sq0).astype(BF16).astype(F32)
+        extended = jnp.where(col == SQ0, sq0, 0.0)
+        extended = jnp.where(col == SQ1, sq1, extended)
+        return jnp.where(
+            col < width, means, jnp.where(col == SQ2, squares - sq0 - sq1, extended)
+        )
+
+    def embed_copy(d):
+        return remote(
+            pack_rows.at[p], pack_rows.at[p], e_send.at[d], e_recv.at[p], {"pack": (p + d) % n_pack}
+        )
 
     def slot(s, carry):
         @pl.when(s == 1)
         def _():
             take_near(2, True)
-            own_to_far(last).start()
 
         @pl.when(s == 2)
         def _():
@@ -266,49 +311,33 @@
             got(s, 3, rows.at[s, far]).wait_recv()
 
         share(s, far, 7).start()
-        for k, offset in ((2, chip), (4, left // 2), (5, right // 2), (7, far // 2)):
-            got(s, k, rows.at[s, offset * 2 + 1 - core]).wait_recv()
-        attend(s)
+
+        @pl.when(s == last)
+        def _():
+            pack_rows[p] = (image_rows() + marks[...]).astype(BF16)
+            for d in far_first(n_pack):
+                embed_copy(d).start()
+
+        for k, whose in ((2, chip), (4, left // 2), (5, right // 2)):
+            got(s, k, rows.at[s, whose * 2 + 1 - core]).wait_recv()
+        near = project(s, (chip, left // 2, right // 2))
+        got(s, 7, rows.at[s, far + 1 - 2 * core]).wait_recv()
+        attend(s, near + project(s, (far // 2,)))
         return carry
 
     lax.fori_loop(0, SRC, slot, 0)
 
-    r = iota((SRC * IPB, 1), 0)
-    label = jnp.zeros((SRC * IPB, 1), jnp.int32)
-    place = jnp.zeros((SRC * IPB, 1), jnp.int32)
-    count = jnp.ones((SRC * IPB, 1), jnp.int32)
-    for s in range(SRC):
-        for n in range(IPB):
-            here = r == s * IPB + n
-            label = jnp.where(here, info_ref[s, 1 + IPB + n], label)
-            place = jnp.where(here, info_ref[s, 0] * IPB + n, place)
-            count = jnp.where(here, info_ref[s, 1 + n], count)
-    embeds = (pooled[...] * (1.0 / count.astype(F32))).astype(BF16)
-    squares = jnp.sum(embeds.astype(F32) * embeds.astype(F32), axis=1, keepdims=True)
-    sq0 = squares.astype(BF16).astype(F32)
-    sq1 = (squares - sq0).astype(BF16).astype(F32)
-    sq2 = squares - sq0 - sq1
-    col = iota((SRC * IPB, 256), 1)
-    extended = jnp.zeros((SRC * IPB, 256), F32)
-    for at, value in (
-        (LABEL_HI, (label // 8).astype(F32)),
-        (LABEL_LO, (label % 8).astype(F32)),
-        (PLACE, place.astype(F32)),
-        (SQ0, sq0),
-        (SQ1, sq1),
-        (SQ2, sq2),
-    ):
-        extended = jnp.where(col == at, value, extended)
-    pack_rows[p] = extended.astype(BF16)
-    pack_rows[p, :, 0:width] = embeds
-
-    def embed_copy(d):
+    whole = image_rows()
+    late_rows[p, 0:IPB, :] = whole[last * IPB :, 0:128]
+    late_rows[p, IPB : 2 * IPB, :] = whole[last * IPB :, 128:256]
+
+    def late_copy(d):
         return remote(
-            pack_rows.at[p], pack_rows.at[p], e_send.at[d], e_recv.at[p], {"pack": (p + d) % n_pack}
+            late_rows.at[p], late_rows.at[p], l_send.at[d], l_recv.at[p], {"pack": (p + d) % n_pack}
         )
 
     for d in far_first(n_pack):
-        embed_copy(d).start()
+        late_copy(d).start()
 
     for d in range(1, n_dp):
         src = (g + d) % n_dp
@@ -339,7 +368,25 @@
     loose = pack_rows[...].reshape(n_slots, 256)
     find = jnp.where(iota((128, 256), 1) == PLACE, 1.0, 0.0).astype(BF16)
     placing = dot_t(find, loose) == iota((128, n_slots), 0).astype(F32)
-    packed = dot(jnp.where(placing, 1.0, 0.0).astype(BF16), loose).astype(BF16)
+    placing = jnp.where(placing, 1.0, 0.0).astype(BF16)
+    early = dot(placing, loose)
+    slot_row = iota((n_slots, n_pack * 8), 0)
+    late_row = iota((n_slots, n_pack * 8), 1)
+    pair = (slot_row // 16 == late_row // 8) & (slot_row % 16 >= last * IPB)
+    pair = pair & (slot_row % IPB == late_row % IPB)
+    first = late_row % 8 < IPB
+    first_placing = dot(placing, jnp.where(pair & first, 1.0, 0.0).astype(BF16)).astype(BF16)
+    second_placing = dot(placing, jnp.where(pair & jnp.logical_not(first), 1.0, 0.0).astype(BF16))
+    second_placing = second_placing.astype(BF16)
+
+    for d in range(1, n_pack):
+        src = (p + d) % n_pack
+        remote(
+            late_rows.at[src], late_rows.at[src], l_send.at[d], l_recv.at[src], {"pack": src}
+        ).wait_recv()
+    late = late_rows[...].reshape(n_pack * 8, 128).astype(BF16)
+    late = jnp.concatenate([dot(first_placing, late), dot(second_placing, late)], axis=1)
+    packed = (early + late).astype(BF16)
 
     products = dot_t(left_side, packed)
     image_lane = iota((n_texts, 128), 1)
@@ -433,6 +480,7 @@
         text_term_copy(d).wait_send()
     for d in range(1, n_pack):
         embed_copy(d).wait_send()
+        late_copy(d).wait_send()
         image_copy(d).wait_send()
     for k in range(3):
         sims_copy(k).wait_send()
@@ -455,9 +503,9 @@
     width = caption_vectors.shape[1]
     depth = attention_projections.shape[1]
     n_texts = n_dp * caption_vectors.shape[0]
-    block_info = jnp.concatenate(
-        [slot_destinations[:, None], tokens_per_picture, caption_indices], axis=1
-    )
+    block_info = jnp.pad(tokens_per_picture, ((0, SRC), (0, 128 - IPB)))
+    block_info += jnp.pad(caption_indices, ((SRC, 0), (0, 128 - IPB)))
+    block_info += jnp.pad(slot_destinations[None, :], ((0, 2 * SRC - 1), (IPB, 128 - IPB - SRC)))
     vmem = pl.BlockSpec(memory_space=pltpu.VMEM)
     hbm = pl.BlockSpec(memory_space=pltpu.HBM)
     dma = pltpu.SemaphoreType.DMA
@@ -475,9 +523,12 @@
             pltpu.SMEM((1,), F32),
             pltpu.VMEM((3, width, depth), BF16),
             pltpu.VMEM((SRC, n_mp, width, BLK), BF16),
-            pltpu.VMEM((SRC * IPB, width), F32),
+            pltpu.VMEM((SRC * IPB, 256), F32),
             pltpu.VMEM((n_dp, 8, 256), F32),
             pltpu.VMEM((n_pack, SRC * IPB, 256), BF16),
+            pltpu.VMEM((n_pack, 8, 128), F32),
+            pltpu.VMEM((SRC * IPB, 256), F32),
+            pltpu.VMEM((SRC * IPB, 256), F32),
             pltpu.VMEM((n_mp, n_texts + 8, 128), F32),
             pltpu.VMEM((2, n_texts + 8, 128), F32),
             pltpu.VMEM((n_dp, 8, 256), F32),
@@ -489,6 +540,8 @@
             dma((SRC, 9)),
             dma((n_dp,)),
             dma((n_dp,)),
+            dma((n_pack,)),
+            dma((n_pack,)),
             dma((n_pack,)),
             dma((n_pack,)),
             dma((4,)),

time: 66.9 us -> 66.1 us (0.988)
  local copies, waits for them, and re-layouts: 2.63 us -> 1.89 us
    add x0 -> x1, other arithmetic: none -> 0.79 us  [on_device(): block_info += jnp.pad(slot_destinations[None, :], ((0, 2 * SRC - 1), (IPB...]
    concatenate x1 -> x0, other arithmetic: 0.77 us -> none  [on_device(): jnp.concatenate([slot_destinations[:, None], tokens_per_picture, caption_...]
    broadcast_in_dim x1 -> x0, local copies, waits for them, and re-layouts: 0.74 us -> none  [on_device(): slot_destinations[:, None]]
where the time goes in v3:
time: 66.1 us; the launch traced here: 65.9 us
  Pallas kernels  61.3 us (93%)
  between operations  1.93 us (3%)
  local copies, waits for them, and re-layouts  1.89 us (3%)
  other arithmetic  0.79 us (1%)
    pallas_call x1, Pallas kernels, on_device(): pl.pallas_call(functools.partial(kernel, n_dp, n_pack, n_mp), out_shape=(...  61.3 us
    unnamed x4, local copies, waits for them, and re-layouts  1.89 us

profile of v3, /device:TPU:1, one launch (start us, length us, event | category | flops | bytes accessed | tf_op | source)
XLA Modules:
  0.0 65.9 jit_solution(14093078184681176431)
XLA Ops:
  1.9 0.8 %pad_add_fusion.info_hbm = s32[8,128]{1,0:T(8,128)S(1)} fusion(s32[1,4]{1,0:T(1,128)} %bitcast.5, s32[4,4]{1,0:T(4,128)} %param.11, s32[4,4]{1,0:T(4,128)} %param.9), kind=kLoop, calls=%fused_computation | loop fusion | flops 2048 | bytes 4240 | tf_op jit(solution)/shard_map/add | solution.py:508
  2.7 0.0 copy-start
  2.7 0.7 %copy-done = bf16[8,192]{1,0:T(8,128)(2,1)S(1)} copy-done((bf16[8,192]{1,0:T(8,128)(2,1)S(1)}, bf16[8,192]{1,0:T(8,128)(2,1)}, u32[]{:S(2)}) %copy-start) | copy-done | bytes 3096
  3.4 61.3 %contrastive_step.1 = (f32[8,192]{1,0:T(8,128)S(1)}, f32[8,192]{1,0:T(8,128)S(1)}) custom-call(bf16[4,192,256]{2,1,0:T(8,128)(2,1)} %bitcast.4, s32[8,128]{1,0:T(8,128)S(1)} %pad_add_fusion.info_hbm, bf16[3,192,1536]{2,1,0:T(8,128)(2,1)} %bitcast.3, bf16[8,192]{1,0:T(8,128)(2,1)S(1)} %copy-done, f32[1]{0:T(128)S(6)} %copy.12.heat_hbm, f32[1]{0:T(128)S(6)} %copy.13.shift_hbm), custom_call_target="tpu_custom_call" | custom-call | tf_op jit(solution)/shard_map/contrastive_step/pallas_call | solution.py:512
  64.7 0.6 copy.14
  65.3 0.6 copy.15
Async XLA Ops:
  2.7 0.7 %copy-start = (bf16[8,192]{1,0:T(8,128)(2,1)S(1)}, bf16[8,192]{1,0:T(8,128)(2,1)}, u32[]{:S(2)}) copy-start(bf16[8,192]{1,0:T(8,128)(2,1)} %texts_ref.1) | copy-start | bytes 9220

commit v4 on v3

--- a/solution.py
+++ b/solution.py
@@ -50,8 +50,7 @@
     texts_ref,
     heat_hbm,
     shift_hbm,
-    image_out,
-    text_out,
+    out,
     info_ref,
     heat_ref,
     shift_ref,
@@ -455,13 +454,13 @@
         remote(
             own_text.at[src], text_terms.at[src], ty_send.at[d], ty_recv.at[src], {"dp": src}
         ).wait_recv()
-    text_out[...] = jnp.sum(text_terms[...], axis=0)[:, 0:width]
+    out[1] = jnp.sum(text_terms[...], axis=0)[:, 0:width]
     for d in range(1, n_pack):
         src = (p + d) % n_pack
         remote(
             own_image.at[src], image_terms.at[src], iz_send.at[d], iz_recv.at[src], {"pack": src}
         ).wait_recv()
-    image_out[...] = jnp.sum(image_terms[...], axis=0)[:, 0:width]
+    out[0] = jnp.sum(image_terms[...], axis=0)[:, 0:width]
 
     for s in range(SRC):
         own_to_right(s).wait_send()
@@ -509,14 +508,11 @@
     vmem = pl.BlockSpec(memory_space=pltpu.VMEM)
     hbm = pl.BlockSpec(memory_space=pltpu.HBM)
     dma = pltpu.SemaphoreType.DMA
-    return pl.pallas_call(
+    grads = pl.pallas_call(
         functools.partial(kernel, n_dp, n_pack, n_mp),
-        out_shape=(
-            jax.ShapeDtypeStruct(caption_vectors.shape, F32),
-            jax.ShapeDtypeStruct(caption_vectors.shape, F32),
-        ),
+        out_shape=jax.ShapeDtypeStruct((2, *caption_vectors.shape), F32),
         in_specs=[hbm, hbm, hbm, vmem, hbm, hbm],
-        out_specs=(vmem, vmem),
+        out_specs=vmem,
         scratch_shapes=[
             pltpu.SMEM(block_info.shape, jnp.int32),
             pltpu.SMEM((1,), F32),
@@ -563,6 +559,7 @@
         score_inverse_heat,
         score_shift,
     )
+    return grads[0], grads[1]
 
 
 def solution(mesh):

time: 66.1 us -> 65.5 us (level)
    unnamed x4 -> x2, local copies, waits for them, and re-layouts: 1.89 us -> 0.69 us
where the time goes in v4:
time: 65.5 us; the launch traced here: 65.3 us
  Pallas kernels  61.3 us (94%)
  between operations  1.93 us (3%)
  local copies, waits for them, and re-layouts  1.29 us (2%)
  other arithmetic  0.79 us (1%)
    pallas_call x1, Pallas kernels, on_device(): pl.pallas_call(functools.partial(kernel, n_dp, n_pack, n_mp), out_shape=j...  61.3 us

profile of v4, /device:TPU:1, one launch (start us, length us, event | category | flops | bytes accessed | tf_op | source)
XLA Modules:
  0.0 65.3 jit_solution(7140287269967818035)
XLA Ops:
  1.9 0.8 %pad_add_fusion.info_hbm = s32[8,128]{1,0:T(8,128)S(1)} fusion(s32[1,4]{1,0:T(1,128)} %bitcast.9, s32[4,4]{1,0:T(4,128)} %param.11, s32[4,4]{1,0:T(4,128)} %param.9), kind=kLoop, calls=%fused_computation.2 | loop fusion | flops 2048 | bytes 4240 | tf_op jit(solution)/shard_map/add | solution.py:507
  2.7 0.0 copy-start
  2.7 0.7 %copy-done = bf16[8,192]{1,0:T(8,128)(2,1)S(1)} copy-done((bf16[8,192]{1,0:T(8,128)(2,1)S(1)}, bf16[8,192]{1,0:T(8,128)(2,1)}, u32[]{:S(2)}) %copy-start) | copy-done | bytes 3096
  3.4 61.3 %contrastive_step.1 = f32[2,8,192]{2,1,0:T(8,128)S(1)} custom-call(bf16[4,192,256]{2,1,0:T(8,128)(2,1)} %bitcast.8, s32[8,128]{1,0:T(8,128)S(1)} %pad_add_fusion.info_hbm, bf16[3,192,1536]{2,1,0:T(8,128)(2,1)} %bitcast.7, bf16[8,192]{1,0:T(8,128)(2,1)S(1)} %copy-done, f32[1]{0:T(128)S(6)} %copy.10.heat_hbm, f32[1]{0:T(128)S(6)} %copy.11.shift_hbm), custom_call_target="tpu_custom_call" | custom-call | tf_op jit(solution)/shard_map/contrastive_step/pallas_call | solution.py:511
  64.7 0.6 slice_bitcast_fusion
Async XLA Ops:
  2.7 0.7 %copy-start = (bf16[8,192]{1,0:T(8,128)(2,1)S(1)}, bf16[8,192]{1,0:T(8,128)(2,1)}, u32[]{:S(2)}) copy-start(bf16[8,192]{1,0:T(8,128)(2,1)} %texts_ref.1) | copy-start | bytes 9220

commit v5 on v4

--- a/solution.py
+++ b/solution.py
@@ -425,7 +425,11 @@
     contract0 = (((0,), (0,)), ((), ()))
     image_part = lax.dot_general(hi, text_bf, contract0, preferred_element_type=F32)
     image_part += lax.dot_general(lo, text_bf, contract0, preferred_element_type=F32)
-    own_image[...] = image_part[0:n_images].reshape(n_pack, 8, 256)
+    for to in range(n_pack):
+        part = image_part[to * 8 : to * 8 + 8]
+        own_image[to, 0] = part[0:4, 0:128]
+        own_image[to, 1] = part[4:8, 0:128]
+        own_image[to, 2] = jnp.concatenate([part[0:4, 128:192], part[4:8, 128:192]], axis=1)
 
     def image_copy(d):
         to = (p + d) % n_pack
@@ -460,7 +464,11 @@
         remote(
             own_image.at[src], image_terms.at[src], iz_send.at[d], iz_recv.at[src], {"pack": src}
         ).wait_recv()
-    out[0] = jnp.sum(image_terms[...], axis=0)[:, 0:width]
+    pieces = jnp.sum(image_terms[...], axis=0)
+    out[0, 0:4, 0:128] = pieces[0]
+    out[0, 4:8, 0:128] = pieces[1]
+    out[0, 0:4, 128:192] = pieces[2, :, 0:64]
+    out[0, 4:8, 128:192] = pieces[2, :, 64:128]
 
     for s in range(SRC):
         own_to_right(s).wait_send()
@@ -528,9 +536,9 @@
             pltpu.VMEM((n_mp, n_texts + 8, 128), F32),
             pltpu.VMEM((2, n_texts + 8, 128), F32),
             pltpu.VMEM((n_dp, 8, 256), F32),
-            pltpu.VMEM((n_pack, 8, 256), F32),
+            pltpu.VMEM((n_pack, 3, 4, 128), F32),
             pltpu.VMEM((n_dp, 8, 256), F32),
-            pltpu.VMEM((n_pack, 8, 256), F32),
+            pltpu.VMEM((n_pack, 3, 4, 128), F32),
             dma((5,)),
             dma((SRC, 9)),
             dma((SRC, 9)),

time: 65.5 us -> 65.3 us (level)
  no operation moved by 1% of the time
where the time goes in v5:
time: 65.3 us; the launch traced here: 65.1 us
  Pallas kernels  61.1 us (94%)
  between operations  1.93 us (3%)
  local copies, waits for them, and re-layouts  1.29 us (2%)
  other arithmetic  0.79 us (1%)
    pallas_call x1, Pallas kernels, on_device(): pl.pallas_call(functools.partial(kernel, n_dp, n_pack, n_mp), out_shape=j...  61.1 us

profile of v5, /device:TPU:1, one launch (start us, length us, event | category | flops | bytes accessed | tf_op | source)
XLA Modules:
  0.0 65.1 jit_solution(8193087906165188984)
XLA Ops:
  1.9 0.8 %pad_add_fusion.info_hbm = s32[8,128]{1,0:T(8,128)S(1)} fusion(s32[1,4]{1,0:T(1,128)} %bitcast.9, s32[4,4]{1,0:T(4,128)} %param.11, s32[4,4]{1,0:T(4,128)} %param.9), kind=kLoop, calls=%fused_computation.2 | loop fusion | flops 2048 | bytes 4240 | tf_op jit(solution)/shard_map/add | solution.py:515
  2.7 0.0 copy-start
  2.7 0.7 %copy-done = bf16[8,192]{1,0:T(8,128)(2,1)S(1)} copy-done((bf16[8,192]{1,0:T(8,128)(2,1)S(1)}, bf16[8,192]{1,0:T(8,128)(2,1)}, u32[]{:S(2)}) %copy-start) | copy-done | bytes 3096
  3.4 61.1 %contrastive_step.1 = f32[2,8,192]{2,1,0:T(8,128)S(1)} custom-call(bf16[4,192,256]{2,1,0:T(8,128)(2,1)} %bitcast.8, s32[8,128]{1,0:T(8,128)S(1)} %pad_add_fusion.info_hbm, bf16[3,192,1536]{2,1,0:T(8,128)(2,1)} %bitcast.7, bf16[8,192]{1,0:T(8,128)(2,1)S(1)} %copy-done, f32[1]{0:T(128)S(6)} %copy.10.heat_hbm, f32[1]{0:T(128)S(6)} %copy.11.shift_hbm), custom_call_target="tpu_custom_call" | custom-call | tf_op jit(solution)/shard_map/contrastive_step/pallas_call | solution.py:519
  64.5 0.6 slice_bitcast_fusion
Async XLA Ops:
  2.7 0.7 %copy-start = (bf16[8,192]{1,0:T(8,128)(2,1)S(1)}, bf16[8,192]{1,0:T(8,128)(2,1)}, u32[]{:S(2)}) copy-start(bf16[8,192]{1,0:T(8,128)(2,1)} %texts_ref.1) | copy-start | bytes 9220
